TPU v7x, 32 devices: a whole 2x2x4 slice. The times are simulated.
32 devices in a mesh: face: 4 (over y, core), tile: 8 (over z, x).
Axes of the slice: x: 2, y: 2, z: 4, core: 2. Of those that a mesh axis runs over, the one named last changes fastest.
Arguments:
- field: bfloat16 [4, 128, 256, 256], P('face', None, 'tile'), may hold values from -6 to 6
- conv_weight: bfloat16 [9, 256, 256], replicated, may hold values from -0.125 to 0.125
- norm_gain: float32 [256], replicated, may hold values from 0.5 to 1.5
- filter_gain: float32 [2, 256], replicated, may hold values from -1 to 1
- seam_face: int32 [4, 2], replicated, may hold values from 0 to 3
- seam_code: int32 [4, 2], replicated, may hold values from 0 to 3
Outputs:
- filtered: bfloat16 [4, 128, 256, 256], P('face', None, 'tile')
All inputs are finite; a program needn't handle non-finite values.
Results may differ from a plain program's by a relative error of at most 0.0056.
Values may be sent and summed in bfloat16 or wider, within the bound.
A program may use at most 128 MiB of HBM per device.

v0:
```python
import jax
import jax.numpy as jnp
from jax import lax
from jax.sharding import PartitionSpec as P


def with_halo(cells, sides, width):
    for axis, dim in sides:
        count = lax.axis_size(axis)
        head = lax.slice_in_dim(cells, 0, width, axis=dim)
        tail = lax.slice_in_dim(cells, cells.shape[dim] - width, cells.shape[dim], axis=dim)
        cells = jnp.concatenate(
            [
                lax.ppermute(tail, axis, [(i, (i + 1) % count) for i in range(count)]),
                cells,
                lax.ppermute(head, axis, [((i + 1) % count, i) for i in range(count)]),
            ],
            axis=dim,
        )
    return cells


def seam_strip(edges, source, code):
    strip = lax.dynamic_index_in_dim(edges, source * 2 + code % 2, 0, keepdims=False)
    return jnp.where(code >= 2, strip[::-1], strip)


def build_table(length, modes):
    places = lax.iota(jnp.int32, length)
    waves = lax.iota(jnp.int32, modes)
    phase = places[:, None] * waves[None, :] % length
    angle = phase.astype(jnp.float32) * (2.0 * jnp.pi / length)
    return jnp.concatenate([jnp.cos(angle), jnp.sin(angle)], axis=1).astype(jnp.bfloat16)


def filter_cycles(cycles, filter_gain):
    count, length, chan = cycles.shape
    modes = filter_gain.shape[1]
    block = min(modes, 256)
    table = build_table(length, modes)
    correction = jnp.zeros(cycles.shape, jnp.float32)
    for start in range(0, modes, block):
        waves = start + lax.iota(jnp.int32, block)
        part = jnp.concatenate(
            [table[:, start : start + block], table[:, modes + start : modes + start + block]],
            axis=1,
        )
        coeffs = jnp.einsum("lm,klc->kmc", part, cycles, preferred_element_type=jnp.float32)
        cos_part, sin_part = (coeffs[:, :block], coeffs[:, block:])
        real_gain = filter_gain[0, start : start + block][None, :, None]
        imag_gain = filter_gain[1, start : start + block][None, :, None]
        weight = (jnp.where(waves == 0, 1.0, 2.0) / length).astype(jnp.float32)[None, :, None]
        held_real = ((real_gain * cos_part + imag_gain * sin_part) * weight).astype(jnp.bfloat16)
        held_imag = ((imag_gain * cos_part - real_gain * sin_part) * weight).astype(jnp.bfloat16)
        stacked = jnp.concatenate([held_real, -held_imag], axis=1)
        correction = correction + jnp.einsum(
            "lm,kmc->klc", part, stacked, preferred_element_type=jnp.float32
        )
    return (cycles.astype(jnp.float32) + correction).astype(jnp.bfloat16)


def per_device(field, conv_weight, norm_gain, filter_gain, seam_face, seam_code):
    block_in = field[0]
    rows, width, chan = block_in.shape
    tiles = lax.axis_size("tile")
    faces = lax.axis_size("face")
    devices = tiles * faces
    tile_id = lax.axis_index("tile")
    face_id = lax.axis_index("face")
    padded = with_halo(block_in, (("tile", 1),), 1)
    first = tile_id == 0
    last = tile_id == tiles - 1
    face_start = jnp.where(first, block_in[:, 0], padded[:, -1])
    face_end = jnp.where(last, block_in[:, -1], padded[:, 0])
    edges = lax.all_gather(jnp.stack([face_start, face_end]), "face", axis=0, tiled=True)
    left = seam_strip(edges, seam_face[face_id, 0], seam_code[face_id, 0])
    right = seam_strip(edges, seam_face[face_id, 1], seam_code[face_id, 1])
    padded = padded.at[:, 0].set(jnp.where(first, left, padded[:, 0]))
    padded = padded.at[:, -1].set(jnp.where(last, right, padded[:, -1]))
    framed = jnp.pad(padded, ((1, 1), (0, 0), (0, 0)))
    total = jnp.zeros((rows, width, chan), jnp.float32)
    for tap in range(9):
        row_off, col_off = (tap // 3, tap % 3)
        window = framed[row_off : row_off + rows, col_off : col_off + width, :]
        total = total + jnp.einsum(
            "rwc,cd->rwd", window, conv_weight[tap], preferred_element_type=jnp.float32
        )
    centered = total - jnp.mean(total, axis=2, keepdims=True)
    variance = jnp.mean(centered * centered, axis=2, keepdims=True)
    normed = centered / jnp.sqrt(variance + 1e-05) * norm_gain
    mixed = (block_in.astype(jnp.float32) + jax.nn.gelu(normed)).astype(jnp.bfloat16)
    owned = rows // devices
    grouped = mixed.reshape(devices, owned, width, chan)
    done = filter_cycles(
        lax.all_to_all(grouped, ("face", "tile"), split_axis=0, concat_axis=2, tiled=True)[0],
        filter_gain,
    )
    count = done.shape[0]
    split = done.reshape(count, devices, width, chan)
    back = lax.all_to_all(split, ("face", "tile"), split_axis=1, concat_axis=1, tiled=True)
    result = jnp.swapaxes(back, 0, 1)
    out = result.reshape(rows, width, chan)
    return out[None]


def solution(mesh):
    placed = (P("face", None, "tile", None), P(), P(), P(), P(), P())
    return jax.shard_map(
        per_device,
        mesh=mesh,
        in_specs=placed,
        out_specs=P("face", None, "tile", None),
        check_vma=False,
    )
```

profile of v0, /device:TPU:0, one launch (start us, length us, event | category | flops | bytes accessed | tf_op | source)
XLA Modules:
  0.0 189.7 jit_solution(3968553124737604760)
XLA Ops:
  0.0 2.8 %copy.33 = bf16[1,128,32,256]{3,1,2,0:T(8,128)(2,1)S(1)} copy(bf16[1,128,32,256]{3,2,1,0:T(8,128)(2,1)} %param.10) | data formatting | bytes 4194304 | tf_op args[0]
  2.8 6.0 %collective-permute-start.1 = (bf16[128,1,256]{2,0,1:T(8,128)(2,1)S(1)}, bf16[128,1,256]{2,0,1:T(8,128)(2,1)S(1)}, u32[]{:S(2)}, u32[]{:S(2)}) collective-permute-start(bf16[128,1,256]{2,0,1:T(8,128)(2,1)S(1)} %slice.149), channel_id=1, source_target_pairs={{1,0},{2,1},{3,2},{4,3},{5,4},{6,5},{7,6},{0,7},{9,8},{10,9},{11,1... | collective-permute-start | bytes 196616 | tf_op jit(solution)/shard_map/ppermute | solution.py:16
  8.8 1.9 %collective-permute-done.1 = bf16[128,1,256]{2,0,1:T(8,128)(2,1)S(1)} collective-permute-done((bf16[128,1,256]{2,0,1:T(8,128)(2,1)S(1)}, bf16[128,1,256]{2,0,1:T(8,128)(2,1)S(1)}, u32[]{:S(2)}, u32[]{:S(2)}) %collective-permute-start.1) | collective-permute-done | bytes 65568 | tf_op jit(solution)/shard_map/ppermute | solution.py:16
  10.8 0.3 collective-permute-start
  11.0 0.0 copy-done.8
  11.0 0.0 copy-done.9
  11.0 0.7 constant_dynamic-slice_fusion.2
  18.0 0.1 collective-permute-done
  18.2 7.2 %all_gather.3 = bf16[8,128,256]{2,1,0:T(8,128)(2,1)S(1)} all-gather(bf16[2,128,256]{2,1,0:T(8,128)(2,1)S(1)} %pad_maximum_fusion.1), channel_id=1, replica_groups=mesh['face'=4,'tile'=8] {'face'}, dimensions={0}, use_global_device_ids=true | all-gather | bytes 655360 | tf_op jit(solution)/shard_map/all_gather | solution.py:75
  25.4 0.7 rev.6
  26.1 0.7 rev.7
  26.7 0.3 pad_maximum_fusion
  27.0 0.5 copy-done.5
  27.6 0.0 copy-done.4
  27.7 0.4 copy-done.3
  28.1 0.7 fusion.10
  28.8 2.7 %fusion.12 = f32[128,32,256]{2,0,1:T(8,128)} fusion(bf16[128,34,256]{2,0,1:T(8,128)(2,1)S(1)} %fusion.60, bf16[9,256,256]{2,1,0:T(8,128)(2,1)S(1)} %copy-done.3), kind=kOutput, calls=%fused_computation.18 | convolution fusion | flops 536870912 | bytes 6553600 | tf_op jit(solution)/shard_map/rwc,cd->rwd/dot_general | solution.py:85
  31.5 2.7 %fusion.14 = f32[128,32,256]{2,0,1:T(8,128)} fusion(bf16[128,34,256]{2,0,1:T(8,128)(2,1)S(1)} %fusion.60, bf16[9,256,256]{2,1,0:T(8,128)(2,1)S(1)} %copy-done.3), kind=kOutput, calls=%fused_computation.20 | convolution fusion | flops 536870912 | bytes 6553600 | tf_op jit(solution)/shard_map/rwc,cd->rwd/dot_general | solution.py:85
  34.2 2.7 %fusion.16 = f32[128,32,256]{2,0,1:T(8,128)} fusion(bf16[128,34,256]{2,0,1:T(8,128)(2,1)S(1)} %fusion.60, bf16[9,256,256]{2,1,0:T(8,128)(2,1)S(1)} %copy-done.3), kind=kOutput, calls=%fused_computation.22 | convolution fusion | flops 536870912 | bytes 6553600 | tf_op jit(solution)/shard_map/rwc,cd->rwd/dot_general | solution.py:85
  36.9 2.7 %fusion.18 = f32[128,32,256]{2,0,1:T(8,128)} fusion(bf16[128,34,256]{2,0,1:T(8,128)(2,1)S(1)} %fusion.60, bf16[9,256,256]{2,1,0:T(8,128)(2,1)S(1)} %copy-done.3), kind=kOutput, calls=%fused_computation.24 | convolution fusion | flops 536870912 | bytes 6553600 | tf_op jit(solution)/shard_map/rwc,cd->rwd/dot_general | solution.py:85
  39.5 2.7 %fusion.20 = f32[128,32,256]{2,0,1:T(8,128)} fusion(bf16[128,34,256]{2,0,1:T(8,128)(2,1)S(1)} %fusion.60, bf16[9,256,256]{2,1,0:T(8,128)(2,1)S(1)} %copy-done.3), kind=kOutput, calls=%fused_computation.26 | convolution fusion | flops 536870912 | bytes 6553600 | tf_op jit(solution)/shard_map/rwc,cd->rwd/dot_general | solution.py:85
  42.2 2.7 %fusion.42 = f32[128,32,256]{2,0,1:T(8,128)} fusion(bf16[128,34,256]{2,0,1:T(8,128)(2,1)S(1)} %fusion.60, bf16[9,256,256]{2,1,0:T(8,128)(2,1)S(1)} %copy-done.3), kind=kOutput, calls=%fused_computation.58 | convolution fusion | flops 536870912 | bytes 6553600 | tf_op jit(solution)/shard_map/rwc,cd->rwd/dot_general | solution.py:85
  44.9 2.6 %fusion.44 = f32[128,32,256]{2,0,1:T(8,128)} fusion(bf16[128,34,256]{2,0,1:T(8,128)(2,1)S(1)} %fusion.60, bf16[9,256,256]{2,1,0:T(8,128)(2,1)S(1)} %copy-done.3), kind=kOutput, calls=%fused_computation.60 | convolution fusion | flops 536870912 | bytes 6553600 | tf_op jit(solution)/shard_map/rwc,cd->rwd/dot_general | solution.py:85
  47.5 10.5 %fusion.71 = (f32[128,32]{0,1:T(8,128)S(1)}, f32[128,32,256]{2,0,1:T(8,128)S(1)}) fusion(f32[128,32,256]{2,0,1:T(8,128)S(1)} %fusion.10, f32[128,32,256]{2,0,1:T(8,128)} %fusion.12, f32[128,32,256]{2,0,1:T(8,128)} %fusion.14, bf16[128,34,256]{2,0,1:T(8,128)(2,1)S(1)} %fusion.60, bf16[9,256,256]{2,1,0:T(8,128)(2,1)S(1)} %copy-done.3, ...), kind=kOutput, calls=%fused_computation.101 | convolution fusion | flops 546304000 | bytes 40124416 | tf_op jit(solution)/shard_map/rwc,cd->rwd/dot_general | solution.py:85
  58.0 0.0 copy-start
  58.0 0.0 copy-start.7
  58.1 1.3 multiply_reduce_fusion
  59.4 0.2 copy-done
  59.6 0.0 copy-done.7
  59.6 3.7 %fusion.8 = bf16[128,32,256]{2,0,1:T(8,128)(2,1)S(1)} fusion(f32[128,32,256]{2,0,1:T(8,128)S(1)} %get-tuple-element.40, f32[256]{0:T(256)S(1)} %copy-done.7, f32[128,32]{0,1:T(8,128)S(1)} %add_sqrt_fusion, f32[128,32]{0,1:T(8,128)S(1)} %broadcast_multiply_fusion, bf16[1,128,32,256]{3,2,1,0:T(8,128)(2,1)S(1)} %copy-done), kind=kLoop, calls=%fused_computation.9 | loop fusion | flops 14680064 | bytes 8422400 | tf_op jit(solution)/shard_map/convert_element_type | solution.py:91
  63.3 2.5 %copy.29 = bf16[128,32,256]{2,1,0:T(8,128)(2,1)} copy(bf16[128,32,256]{2,0,1:T(8,128)(2,1)S(1)} %fusion.8) | data formatting | bytes 4194304 | tf_op jit(solution)/shard_map/reshape | solution.py:93
  65.8 6.1 %all-to-all-start = ((bf16[32,4,32,256]{3,2,1,0:T(8,128)(2,1)}), bf16[32,4,32,256]{3,2,1,0:T(8,128)(2,1)S(1)}, u32[]{:S(2)}, u32[]{:S(2)}) async-start(bf16[32,4,32,256]{3,2,1,0:T(8,128)(2,1)} %bitcast.103), calls=%async_computation | async-start | bytes 4194304 | tf_op jit(solution)/shard_map/all_to_all | solution.py:95
  72.0 4.4 %sine_convert_fusion = (bf16[1024,256]{1,0:T(8,128)(2,1)S(1)}, bf16[1024,256]{1,0:T(8,128)(2,1)S(1)}) fusion(), kind=kLoop, calls=%fused_computation.47 | loop fusion | flops 4194304 | bytes 1048576 | tf_op jit(solution)/shard_map/convert.1
  76.3 0.0 copy-done.6
  76.4 45.5 %all-to-all-done = bf16[32,4,32,256]{3,2,1,0:T(8,128)(2,1)S(1)} async-done(((bf16[32,4,32,256]{3,2,1,0:T(8,128)(2,1)}), bf16[32,4,32,256]{3,2,1,0:T(8,128)(2,1)S(1)}, u32[]{:S(2)}, u32[]{:S(2)}) %all-to-all-start) | async-done | bytes 2097184 | tf_op jit(solution)/shard_map/all_to_all | solution.py:95
  121.8 0.2 copy.23
  122.0 0.0 copy-start.1
  122.0 1.3 convolution_bitcast_fusion
  123.3 0.0 copy-done.1
  123.3 1.0 fusion.37
  124.3 1.0 multiply_convert_fusion.1
  125.3 0.0 copy-done.2
  125.3 2.4 %copy.24 = bf16[4,1024,256]{1,2,0:T(8,128)(2,1)} copy(bf16[4,1024,256]{2,1,0:T(8,128)(2,1)S(1)} %bitcast.105) | data formatting | bytes 4194304 | tf_op jit(solution)/shard_map/squeeze | solution.py:95
  127.7 4.5 %fusion.9 = bf16[4,1024,256]{1,2,0:T(8,128)(2,1)} fusion(bf16[4,1024,256]{1,2,0:T(8,128)(2,1)} %copy.24, bf16[4,256,256]{1,2,0:T(8,128)(2,1)} %fusion.37, bf16[4,256,256]{1,2,0:T(8,128)(2,1)} %multiply_convert_fusion.1, bf16[1024,256]{1,0:T(8,128)(2,1)S(1)} %get-tuple-element.43, bf16[1024,256]{1,0:T(8,128)(2,1)S(1)} %get-tuple-element.44), kind=kOutput, calls=%fused_computation.11 | convolution fusion | flops 1081081856 | bytes 6291456 | tf_op jit(solution)/shard_map/lm,kmc->klc/dot_general | solution.py:56
  132.2 2.8 %copy.26 = bf16[4,1024,256]{2,1,0:T(8,128)(2,1)S(1)} copy(bf16[4,1024,256]{1,2,0:T(8,128)(2,1)} %fusion.9) | data formatting | bytes 4194304 | tf_op jit(solution)/shard_map/convert_element_type | solution.py:59
  135.1 0.2 copy.27
  135.3 53.1 %all_to_all.20 = bf16[4,32,32,256]{3,2,0,1:T(8,128)(2,1)S(1)} all-to-all(bf16[4,32,32,256]{3,2,0,1:T(8,128)(2,1)S(1)} %copy.27), channel_id=1, replica_groups=mesh['face'=4,'tile'=8] {'face','tile'}, dimensions={1} | all-to-all | bytes 4194304 | tf_op jit(solution)/shard_map/all_to_all | solution.py:100
  188.4 1.3 copy.37
  (18 shorter events, 0.1 us)
Async XLA Ops:
  0.0 11.0 %copy-start.8 = (s32[4,2]{0,1:T(2,128)S(1)}, s32[4,2]{0,1:T(2,128)}, u32[]{:S(2)}) copy-start(s32[4,2]{0,1:T(2,128)} %param.14) | copy-start | bytes 100
  0.0 11.0 %copy-start.9 = (s32[4,2]{0,1:T(2,128)S(1)}, s32[4,2]{0,1:T(2,128)}, u32[]{:S(2)}) copy-start(s32[4,2]{0,1:T(2,128)} %param.15) | copy-start | bytes 100
  2.8 7.9 %collective-permute-start.1 = (bf16[128,1,256]{2,0,1:T(8,128)(2,1)S(1)}, bf16[128,1,256]{2,0,1:T(8,128)(2,1)S(1)}, u32[]{:S(2)}, u32[]{:S(2)}) collective-permute-start(bf16[128,1,256]{2,0,1:T(8,128)(2,1)S(1)} %slice.149), channel_id=1, source_target_pairs={{1,0},{2,1},{3,2},{4,3},{5,4},{6,5},{7,6},{0,7},{9,8},{10,9},{11,1... | collective-permute-start | bytes 196616 | tf_op jit(solution)/shard_map/ppermute | solution.py:16
  10.8 7.4 %collective-permute-start = (bf16[128,1,256]{2,0,1:T(8,128)(2,1)S(1)}, bf16[128,1,256]{2,0,1:T(8,128)(2,1)S(1)}, u32[]{:S(2)}, u32[]{:S(2)}) collective-permute-start(bf16[128,1,256]{2,0,1:T(8,128)(2,1)S(1)} %get-tuple-element.30), channel_id=1, source_target_pairs={{0,1},{1,2},{2,3},{3,4},{4,5},{5,6},{6,7},{7,0},{8,9},{9,10},{10,1... | collective-permute-start | bytes 196616 | tf_op jit(solution)/shard_map/ppermute | solution.py:14
  26.7 0.8 copy-start.5
  26.7 0.9 copy-start.4
  26.7 1.3 copy-start.3
  58.0 1.6 copy-start
  58.0 1.6 copy-start.7
  65.8 10.5 %copy-start.6 = (f32[2,256]{1,0:T(2,128)S(1)}, f32[2,256]{1,0:T(2,128)}, u32[]{:S(2)}) copy-start(f32[2,256]{1,0:T(2,128)} %param.13) | copy-start | bytes 6148
  65.8 56.0 %all-to-all-start = ((bf16[32,4,32,256]{3,2,1,0:T(8,128)(2,1)}), bf16[32,4,32,256]{3,2,1,0:T(8,128)(2,1)S(1)}, u32[]{:S(2)}, u32[]{:S(2)}) async-start(bf16[32,4,32,256]{3,2,1,0:T(8,128)(2,1)} %bitcast.103), calls=%async_computation | async-start | bytes 4194304 | tf_op jit(solution)/shard_map/all_to_all | solution.py:95
  122.0 1.3 copy-start.1
  123.3 2.0 %copy-start.2 = (bf16[32,4,32,256]{3,2,0,1:T(8,128)(2,1)S(1)}, bf16[32,4,32,256]{3,2,0,1:T(8,128)(2,1)}, u32[]{:S(2)}) copy-start(bf16[32,4,32,256]{3,2,0,1:T(8,128)(2,1)} %copy-done.1) | copy-start | bytes 6291460
where the time goes:
time: 190 us
  blocking collectives  60.3 us (32%)
  waiting for transfers between devices  47.5 us (25%)
  matrix products  35.7 us (19%)
  local copies, waits for them, and re-layouts  15.5 us (8%)
  starting transfers between devices  12.4 us (7%)
  other arithmetic  11.7 us (6%)
  between operations  6.52 us (3%)
    all_to_all x1, blocking collectives, per_device(): lax.all_to_all(split, ('face', 'tile'), split_axis=1, concat_axis=1, tile...  53.1 us
    all_to_all x1, waiting for transfers between devices, per_device(): lax.all_to_all(grouped, ('face', 'tile'), split_axis=0, concat_axis=2, ti...  45.5 us
    dot_general x9, matrix products, per_device(): jnp.einsum('rwc,cd->rwd', window, conv_weight[tap], preferred_element_typ...  29.9 us
    all_gather x1, blocking collectives, per_device(): lax.all_gather(jnp.stack([face_start, face_end]), 'face', axis=0, tiled=T...  7.2 us
    all_to_all x1, starting transfers between devices, per_device(): lax.all_to_all(grouped, ('face', 'tile'), split_axis=0, concat_axis=2, ti...  6.13 us
    ppermute x1, starting transfers between devices, with_halo(): lax.ppermute(head, axis, [((i + 1) % count, i) for i in range(count)])  6.03 us
    unnamed x22, local copies, waits for them, and re-layouts  5.39 us
    dot_general x1, matrix products, filter_cycles(): jnp.einsum('lm,kmc->klc', part, stacked, preferred_element_type=jnp.float32)  4.53 us
  transfers between devices with their start and end apart: 3, of which 3 were waited for; matrix products, arithmetic and copies ran while one was open for 3% of the time, Pallas kernels for 0%

commit v1 on v0

v1 whole, which is shorter than its diff:
```python
import functools

import jax
import jax.numpy as jnp
import numpy as np
from jax import lax
from jax.experimental import pallas as pl
from jax.experimental.pallas import tpu as pltpu
from jax.sharding import PartitionSpec as P

MESH = pl.DeviceIdType.MESH
BF = jnp.bfloat16
F32 = jnp.float32


def make_table(length, modes):
    phase = np.arange(length)[:, None] * np.arange(modes)[None, :] % length
    angle = phase.astype(np.float64) * (2.0 * np.pi / length)
    return np.concatenate([np.cos(angle), np.sin(angle)], axis=1).astype(BF)


def kernel(
    faces,
    tiles,
    x_ref,
    edge_ref,
    w_ref,
    gain_ref,
    fgain_ref,
    table_ref,
    tablet_ref,
    sface_ref,
    scode_ref,
    out_ref,
    seam,
    near,
    halo,
    x3,
    mixed,
    cyc,
    near_send,
    near_recv,
    seam_send,
    seam_recv,
    send1,
    recv1,
    send2,
    recv2,
    self_sem,
):
    rows, width, chan = x_ref.shape
    devices = faces * tiles
    owned = rows // devices
    phases, part = cyc.shape[0], cyc.shape[1]
    length = devices * width
    modes = fgain_ref.shape[1]
    half = tiles // 2
    group = half * owned
    face = lax.axis_index("face")
    tile = lax.axis_index("tile")
    me = face * tiles + tile

    barrier = pltpu.get_barrier_semaphore()

    def peer(k):
        side = k // (faces * half)
        rest = k % (faces * half)
        pf = (face + rest // half) % faces
        pt = ((tile // half + 1 + side) % 2) * half + (tile % half + rest % half) % half
        return pf, pt

    own = devices // 2

    def each_peer(fn):
        def step(k, carry):
            @pl.when(k != own)
            def _():
                pf, pt = peer(k)
                fn(pf, pt)

            return carry

        lax.fori_loop(0, devices, step, 0)

    each_peer(
        lambda pf, pt: pl.semaphore_signal(barrier, inc=1, device_id=(pf, pt), device_id_type=MESH)
    )
    pl.semaphore_wait(barrier, devices - 1)

    def to_right():
        return pltpu.make_async_remote_copy(
            edge_ref.at[1], near.at[0], near_send.at[0], near_recv.at[0],
            device_id=(face, (tile + 1) % tiles), device_id_type=MESH,
        )

    def to_left():
        return pltpu.make_async_remote_copy(
            edge_ref.at[0], near.at[1], near_send.at[1], near_recv.at[1],
            device_id=(face, (tile + tiles - 1) % tiles), device_id_type=MESH,
        )

    def seam_copy(slot, side, k):
        pf = (face + k // 2) % faces
        pt = (tile + (k % 2) * (tiles - 1)) % tiles if side == 0 else (tile + (k % 2)) % tiles
        return pltpu.make_async_remote_copy(
            edge_ref.at[side], seam.at[slot], seam_send.at[k], seam_recv.at[slot],
            device_id=(pf, pt), device_id_type=MESH,
        )

    def seam_local(side):
        return pltpu.make_async_copy(edge_ref.at[side], seam.at[face * 2 + side], seam_recv.at[face * 2 + side])

    for side, end in ((0, 0), (1, tiles - 1)):
        @pl.when(tile == end)
        def _():
            for k in range(1, 2 * faces):
                seam_copy(face * 2 + side, side, k).start()
            seam_local(side).start()

    @pl.when(tile < tiles - 1)
    def _():
        to_right().start()

    @pl.when(tile > 0)
    def _():
        to_left().start()

    x3[0] = jnp.zeros(x3.shape[1:], BF)
    x3[rows + 1] = jnp.zeros(x3.shape[1:], BF)

    @pl.when(tile > 0)
    def _():
        to_right().wait_recv()
        halo[0] = near[0].astype(F32).reshape(rows, 1, chan)

    @pl.when(tile < tiles - 1)
    def _():
        to_left().wait_recv()
        halo[1] = near[1].astype(F32).reshape(rows, 1, chan)

    down = lax.broadcasted_iota(jnp.int32, (rows, rows), 0)
    across = lax.broadcasted_iota(jnp.int32, (rows, rows), 1)
    for side, end in ((0, 0), (1, tiles - 1)):
        @pl.when(tile == end)
        def _():
            for slot in range(2 * faces):
                pltpu.make_async_copy(edge_ref.at[0], seam.at[slot], seam_recv.at[slot]).wait()
            code = scode_ref[face, side]
            strip = seam[sface_ref[face, side] * 2 + code % 2]
            target = jnp.where(code >= 2, rows - 1 - down, down)
            order = jnp.where(target == across, 1.0, 0.0).astype(BF)
            halo[side] = jnp.dot(order, strip, preferred_element_type=F32).reshape(rows, 1, chan)

    batch = 8

    def shift(b, carry):
        at = pl.ds(b * batch, batch)
        dst = pl.ds(b * batch + 1, batch)
        here = x_ref[at]
        wide = here.astype(F32)
        col = lax.broadcasted_iota(jnp.int32, wide.shape, 1)
        x3[dst, :, 0:chan] = jnp.where(col == 0, halo[0, at], pltpu.roll(wide, 1, 1)).astype(BF)
        x3[dst, :, chan : 2 * chan] = here
        x3[dst, :, 2 * chan : 3 * chan] = jnp.where(
            col == width - 1, halo[1, at], pltpu.roll(wide, width - 1, 1)
        ).astype(BF)
        return carry

    lax.fori_loop(0, rows // batch, shift, 0)

    def forward(p, pf, pt):
        d = pf * tiles + pt
        return pltpu.make_async_remote_copy(
            mixed.at[pl.ds(d * owned + p * part, part)],
            cyc.at[p, :, pl.ds(me * width, width), :],
            send1.at[p, d],
            recv1.at[p, me],
            device_id=(pf, pt),
            device_id_type=MESH,
        )

    def forward_wait(p, pf, pt):
        s = pf * tiles + pt
        return pltpu.make_async_remote_copy(
            mixed.at[pl.ds(s * owned + p * part, part)],
            cyc.at[p, :, pl.ds(s * width, width), :],
            send1.at[p, s],
            recv1.at[p, s],
            device_id=(pf, pt),
            device_id_type=MESH,
        )

    def forward_self(p):
        return pltpu.make_async_copy(
            mixed.at[pl.ds(me * owned + p * part, part)],
            cyc.at[p, :, pl.ds(me * width, width), :],
            self_sem.at[0, p],
        )

    gain = gain_ref[...]

    def block(g, carry):
        side = g // faces
        pf = (face + g % faces) % faces
        ph = (tile // half + 1 + side) % 2
        base = (pf * tiles + ph * half) * owned
        total = jnp.zeros((group * width, chan), F32)
        for dy in range(3):
            total += jnp.dot(
                x3[pl.ds(base + dy, group)].reshape(group * width, 3 * chan),
                w_ref[dy],
                preferred_element_type=F32,
            )
        step = group // 4 if group % 4 == 0 else group
        for q in range(group // step):
            piece = total[q * step * width : (q + 1) * step * width]
            centered = piece - jnp.mean(piece, axis=1, keepdims=True)
            variance = jnp.mean(centered * centered, axis=1, keepdims=True)
            normed = centered * (lax.rsqrt(variance + 1e-05)) * gain
            inner = normed * (0.7978845608028654 + 0.035677408136300125 * (normed * normed))
            act = 0.5 * normed * (1.0 + jnp.tanh(inner))
            src = x_ref[pl.ds(base + q * step, step)].astype(F32)
            mixed[pl.ds(base + q * step, step)] = (src + act.reshape(step, width, chan)).astype(BF)

        def push(i, inner_carry):
            pt = ph * half + (tile % half + i) % half

            @pl.when(g * half + i != own)
            def _():
                forward(0, pf, pt).start()

            return inner_carry

        lax.fori_loop(0, half, push, 0)
        return carry

    lax.fori_loop(0, 2 * faces, block, 0)
    for p in range(phases):
        forward_self(p).start()
    for p in range(1, phases):
        each_peer(lambda pf, pt: forward(p, pf, pt).start())

    def back(p, pf, pt):
        d = pf * tiles + pt
        return pltpu.make_async_remote_copy(
            cyc.at[p, :, pl.ds(d * width, width), :],
            out_ref.at[pl.ds(me * owned + p * part, part)],
            send2.at[p, d],
            recv2.at[p, me],
            device_id=(pf, pt),
            device_id_type=MESH,
        )

    def back_wait(p, pf, pt):
        s = pf * tiles + pt
        return pltpu.make_async_remote_copy(
            cyc.at[p, :, pl.ds(s * width, width), :],
            out_ref.at[pl.ds(s * owned + p * part, part)],
            send2.at[p, s],
            recv2.at[p, s],
            device_id=(pf, pt),
            device_id_type=MESH,
        )

    def back_self(p):
        return pltpu.make_async_copy(
            cyc.at[p, :, pl.ds(me * width, width), :],
            out_ref.at[pl.ds(me * owned + p * part, part)],
            self_sem.at[1, p],
        )

    width_m = min(modes, 256)
    eye = lax.broadcasted_iota(jnp.int32, (width_m, width_m), 0) == lax.broadcasted_iota(
        jnp.int32, (width_m, width_m), 1
    )
    stand = lambda row: jnp.sum(jnp.where(eye, row, 0.0), axis=1, keepdims=True)

    def filter_row(p, r):
        held = []
        for start in range(0, modes, width_m):
            waves = start + lax.broadcasted_iota(jnp.int32, (width_m, 1), 0)
            scale = jnp.where(waves == 0, 1.0 / length, 2.0 / length)
            real_gain = stand(fgain_ref[0:1, start : start + width_m]) * scale
            imag_gain = stand(fgain_ref[1:2, start : start + width_m]) * scale
            line = cyc[p, r]
            cos_part = jnp.dot(tablet_ref[start : start + width_m], line, preferred_element_type=F32)
            sin_part = jnp.dot(
                tablet_ref[modes + start : modes + start + width_m], line, preferred_element_type=F32
            )
            held.append(
                (
                    (real_gain * cos_part + imag_gain * sin_part).astype(BF),
                    (real_gain * sin_part - imag_gain * cos_part).astype(BF),
                )
            )
        stacked = jnp.concatenate([h[0] for h in held] + [h[1] for h in held], axis=0)
        piece = 256

        def add(b, carry):
            at = pl.ds(pl.multiple_of(b * piece, piece), piece)
            fix = jnp.dot(table_ref[at], stacked, preferred_element_type=F32)
            cyc[p, r, at] = (cyc[p, r, at].astype(F32) + fix).astype(BF)
            return carry

        lax.fori_loop(0, length // piece, add, 0)

    for p in range(phases):
        each_peer(lambda pf, pt: forward_wait(p, pf, pt).wait_recv())
        forward_self(p).wait()

        def one(r, carry):
            filter_row(p, r)
            return carry

        lax.fori_loop(0, part, one, 0)
        each_peer(lambda pf, pt: back(p, pf, pt).start())
        back_self(p).start()

    @pl.when(tile < tiles - 1)
    def _():
        to_right().wait_send()

    @pl.when(tile > 0)
    def _():
        to_left().wait_send()

    for side, end in ((0, 0), (1, tiles - 1)):
        @pl.when(tile == end)
        def _():
            for k in range(1, 2 * faces):
                seam_copy(face * 2 + side, side, k).wait_send()

    for p in range(phases):
        each_peer(lambda pf, pt: forward(p, pf, pt).wait_send())
    for p in range(phases):
        each_peer(lambda pf, pt: back_wait(p, pf, pt).wait_recv())
        each_peer(lambda pf, pt: back(p, pf, pt).wait_send())
        back_self(p).wait()


def per_device(faces, tiles, field, conv_weight, norm_gain, filter_gain, seam_face, seam_code):
    block_in = field[0]
    rows, width, chan = block_in.shape
    modes = filter_gain.shape[1]
    devices = faces * tiles
    length = devices * width
    owned = rows // devices
    phases = 2 if owned % 2 == 0 else 1
    part = owned // phases
    table = make_table(length, modes)
    edges = jnp.stack([block_in[:, 0], block_in[:, -1]])
    vmem = pl.BlockSpec(memory_space=pltpu.VMEM)
    smem = pl.BlockSpec(memory_space=pltpu.SMEM)
    dma = pltpu.SemaphoreType.DMA
    out = pl.pallas_call(
        functools.partial(kernel, faces, tiles),
        out_shape=jax.ShapeDtypeStruct((rows, width, chan), BF),
        in_specs=[vmem] * 7 + [smem] * 2,
        out_specs=vmem,
        scratch_shapes=[
            pltpu.VMEM((2 * faces, rows, chan), BF),
            pltpu.VMEM((2, rows, chan), BF),
            pltpu.VMEM((2, rows, 1, chan), F32),
            pltpu.VMEM((rows + 2, width, 3 * chan), BF),
            pltpu.VMEM((rows, width, chan), BF),
            pltpu.VMEM((phases, part, length, chan), BF),
            dma((2,)),
            dma((2,)),
            dma((2 * faces,)),
            dma((2 * faces,)),
            dma((phases, devices)),
            dma((phases, devices)),
            dma((phases, devices)),
            dma((phases, devices)),
            dma((2, phases)),
        ],
        compiler_params=pltpu.CompilerParams(
            collective_id=0, has_side_effects=True, vmem_limit_bytes=60 * 1024 * 1024
        ),
    )(
        block_in,
        edges,
        conv_weight.reshape(3, 3 * chan, chan),
        norm_gain.reshape(1, chan),
        filter_gain,
        jnp.asarray(table),
        jnp.asarray(np.ascontiguousarray(table.T)),
        seam_face,
        seam_code,
    )
    return out[None]


def solution(mesh):
    placed = (P("face", None, "tile", None), P(), P(), P(), P(), P())
    return jax.shard_map(
        functools.partial(per_device, mesh.shape["face"], mesh.shape["tile"]),
        mesh=mesh,
        in_specs=placed,
        out_specs=P("face", None, "tile", None),
        check_vma=False,
    )
```

time: 190 us -> 124 us (0.65)
  Pallas kernels: 0 us -> 114 us
  blocking collectives: 60.3 us -> 0 us
  waiting for transfers between devices: 47.5 us -> 0 us
  matrix products: 35.7 us -> 0 us
  starting transfers between devices: 12.4 us -> 0 us
  other arithmetic: 11.7 us -> 0.67 us
  local copies, waits for them, and re-layouts: 15.5 us -> 8.54 us
  between operations: 6.52 us -> 0.02 us
    pallas_call x0 -> x1, Pallas kernels: none -> 114 us  [per_device(): pl.pallas_call(functools.partial(kernel, faces, tiles), out_shape=jax.Sha...]
    all_to_all x1 -> x0, blocking collectives: 53.1 us -> none  [per_device(): lax.all_to_all(split, ('face', 'tile'), split_axis=1, concat_axis=1, tile...]
    all_to_all x1 -> x0, waiting for transfers between devices: 45.5 us -> none  [per_device(): lax.all_to_all(grouped, ('face', 'tile'), split_axis=0, concat_axis=2, ti...]
    dot_general x11 -> x0, matrix products: 35.7 us -> none  [the longest x9 29.9 us: per_device(): jnp.einsum('rwc,cd->rwd', window, conv_weight[tap], preferred_element_typ...]
    all_gather x1 -> x0, blocking collectives: 7.2 us -> none  [per_device(): lax.all_gather(jnp.stack([face_start, face_end]), 'face', axis=0, tiled=T...]
    ppermute x2 -> x0, starting transfers between devices: 6.3 us -> none  [the longest x1 6.03 us: with_halo(): lax.ppermute(head, axis, [((i + 1) % count, i) for i in range(count)])]
    all_to_all x1 -> x0, starting transfers between devices: 6.13 us -> none  [per_device(): lax.all_to_all(grouped, ('face', 'tile'), split_axis=0, concat_axis=2, ti...]
    convert_element_type x2 -> x0, other arithmetic: 4.66 us -> none  [the longest x1 3.67 us: per_device(): (block_in.astype(jnp.float32) + jax.nn.gelu(normed)).astype(jnp.bfloat16)]
  transfers between devices with their start and end apart: 3 -> 0, of which waited for: 3 -> 0; matrix products, arithmetic and copies ran while one was open for 3% -> 0% of each run, Pallas kernels for 0% -> 0%
where the time goes in v1:
time: 124 us; the launch traced here: 123 us
  Pallas kernels  114 us (92%)
  local copies, waits for them, and re-layouts  8.54 us (7%)
    pallas_call x1, Pallas kernels, per_device(): pl.pallas_call(functools.partial(kernel, faces, tiles), out_shape=jax.Sha...  114 us
    unnamed x4, local copies, waits for them, and re-layouts  8.53 us

profile of v1, /device:TPU:0, one launch (start us, length us, event | category | flops | bytes accessed | tf_op | source)
XLA Modules:
  0.0 123.2 jit_solution(6931666012812630064)
XLA Ops:
  0.0 1.3 %copy.11.sface_ref = s32[4,2]{1,0:T(4,128)} copy(s32[4,2]{0,1:T(2,128)} %param.12) | data formatting | bytes 64 | tf_op args[4]
  1.3 1.4 %copy.12.scode_ref = s32[4,2]{1,0:T(4,128)} copy(s32[4,2]{0,1:T(2,128)} %param.13) | data formatting | bytes 64 | tf_op args[5]
  2.7 2.8 %copy.15 = bf16[1,128,32,256]{3,1,2,0:T(8,128)(2,1)S(1)} copy(bf16[1,128,32,256]{3,2,1,0:T(8,128)(2,1)} %param.8) | data formatting | bytes 4194304 | tf_op args[0]
  5.5 0.7 pad_maximum_fusion.edge_ref
  6.1 114.0 %shard_map.82 = bf16[128,32,256]{2,1,0:T(8,128)(2,1)} custom-call(bf16[128,32,256]{2,1,0:T(8,128)(2,1)} %bitcast.11, bf16[2,128,256]{2,1,0:T(8,128)(2,1)} %pad_maximum_fusion.edge_ref, bf16[3,768,256]{2,1,0:T(8,128)(2,1)} %bitcast.14, f32[1,256]{1,0:T(1,128)} %bitcast.15, f32[2,256]{1,0:T(2,128)} %fgain_ref.1, bf16[1024,512]{1,0:T(8,128)(2,1)} %constant.4.clone.table_ref, ...), custom_call_target="tpu_custom_call" | custom-call | tf_op jit(solution)/shard_map/pallas_call | solution.py:355
  120.1 3.1 %copy.17 = bf16[1,128,32,256]{3,2,1,0:T(8,128)(2,1)} copy(bf16[1,128,32,256]{3,2,1,0:T(8,128)(2,1)} %bitcast.12) | data formatting | bytes 4194304
  (1 shorter events, 0.0 us)

commit v2 on v1

--- a/solution.py
+++ b/solution.py
@@ -23,15 +23,18 @@
     faces,
     tiles,
     x_ref,
-    edge_ref,
-    w_ref,
     gain_ref,
     fgain_ref,
-    table_ref,
-    tablet_ref,
+    w_hbm,
+    table_hbm,
+    tablet_hbm,
     sface_ref,
     scode_ref,
     out_ref,
+    w_ref,
+    table_ref,
+    tablet_ref,
+    edge_ref,
     seam,
     near,
     halo,
@@ -47,6 +50,7 @@
     send2,
     recv2,
     self_sem,
+    load_sem,
 ):
     rows, width, chan = x_ref.shape
     devices = faces * tiles
@@ -85,6 +89,22 @@
     each_peer(
         lambda pf, pt: pl.semaphore_signal(barrier, inc=1, device_id=(pf, pt), device_id_type=MESH)
     )
+    loads = [
+        pltpu.make_async_copy(src, dst, load_sem.at[k])
+        for k, (src, dst) in enumerate(
+            ((w_hbm, w_ref), (tablet_hbm, tablet_ref), (table_hbm, table_ref))
+        )
+    ]
+    for load in loads:
+        load.start()
+
+    def pick(b, carry):
+        at = pl.ds(b * 16, 16)
+        edge_ref[0, at] = x_ref[at].astype(F32)[:, 0, :].astype(BF)
+        edge_ref[1, at] = x_ref[at].astype(F32)[:, width - 1, :].astype(BF)
+        return carry
+
+    lax.fori_loop(0, rows // 16, pick, 0)
     pl.semaphore_wait(barrier, devices - 1)
 
     def to_right():
@@ -99,34 +119,30 @@
             device_id=(face, (tile + tiles - 1) % tiles), device_id_type=MESH,
         )
 
-    def seam_copy(slot, side, k):
-        pf = (face + k // 2) % faces
-        pt = (tile + (k % 2) * (tiles - 1)) % tiles if side == 0 else (tile + (k % 2)) % tiles
-        return pltpu.make_async_remote_copy(
-            edge_ref.at[side], seam.at[slot], seam_send.at[k], seam_recv.at[slot],
+    def seam_copy(slot, k, pf, pt):
+        return pltpu.make_async_remote_copy(
+            seam.at[slot], seam.at[slot], seam_send.at[k], seam_recv.at[slot],
             device_id=(pf, pt), device_id_type=MESH,
         )
 
-    def seam_local(side):
-        return pltpu.make_async_copy(edge_ref.at[side], seam.at[face * 2 + side], seam_recv.at[face * 2 + side])
-
-    for side, end in ((0, 0), (1, tiles - 1)):
+    ends = ((0, 0, tiles - 1), (1, tiles - 1, 0))
+
+    @pl.when(tile < tiles - 1)
+    def _():
+        to_right().start()
+
+    @pl.when(tile > 0)
+    def _():
+        to_left().start()
+
+    for side, end, other in ends:
         @pl.when(tile == end)
         def _():
-            for k in range(1, 2 * faces):
-                seam_copy(face * 2 + side, side, k).start()
-            seam_local(side).start()
-
-    @pl.when(tile < tiles - 1)
-    def _():
-        to_right().start()
-
-    @pl.when(tile > 0)
-    def _():
-        to_left().start()
-
-    x3[0] = jnp.zeros(x3.shape[1:], BF)
-    x3[rows + 1] = jnp.zeros(x3.shape[1:], BF)
+            mine = face * 2 + side
+            seam[mine] = edge_ref[side]
+            seam_copy(mine, 0, face, other).start()
+            for k in range(1, faces):
+                seam_copy(mine, k, (face + k) % faces, end).start()
 
     @pl.when(tile > 0)
     def _():
@@ -140,22 +156,25 @@
 
     down = lax.broadcasted_iota(jnp.int32, (rows, rows), 0)
     across = lax.broadcasted_iota(jnp.int32, (rows, rows), 1)
-    for side, end in ((0, 0), (1, tiles - 1)):
+    for side, end, other in ends:
         @pl.when(tile == end)
         def _():
-            for slot in range(2 * faces):
-                pltpu.make_async_copy(edge_ref.at[0], seam.at[slot], seam_recv.at[slot]).wait()
-            code = scode_ref[face, side]
-            strip = seam[sface_ref[face, side] * 2 + code % 2]
+            far = face * 2 + 1 - side
+            seam_copy(far, 0, face, other).wait_recv()
+            for k in range(1, faces):
+                seam_copy(far, faces + k - 1, (face + k) % faces, end).start()
+            for k in range(1, faces):
+                pf = (face + k) % faces
+                seam_copy(pf * 2 + side, k, pf, end).wait_recv()
+                seam_copy(pf * 2 + 1 - side, faces + k - 1, pf, end).wait_recv()
+            code = scode_ref[side, face]
+            strip = seam[sface_ref[side, face] * 2 + code % 2]
             target = jnp.where(code >= 2, rows - 1 - down, down)
             order = jnp.where(target == across, 1.0, 0.0).astype(BF)
             halo[side] = jnp.dot(order, strip, preferred_element_type=F32).reshape(rows, 1, chan)
 
-    batch = 8
-
-    def shift(b, carry):
-        at = pl.ds(b * batch, batch)
-        dst = pl.ds(b * batch + 1, batch)
+    def shift(dst, row, count):
+        at = pl.ds(row, count)
         here = x_ref[at]
         wide = here.astype(F32)
         col = lax.broadcasted_iota(jnp.int32, wide.shape, 1)
@@ -164,9 +183,21 @@
         x3[dst, :, 2 * chan : 3 * chan] = jnp.where(
             col == width - 1, halo[1, at], pltpu.roll(wide, width - 1, 1)
         ).astype(BF)
-        return carry
-
-    lax.fori_loop(0, rows // batch, shift, 0)
+
+    def frame(base):
+        batch = 8 if group % 8 == 0 else group
+        for b in range(0, group, batch):
+            shift(pl.ds(b + 1, batch), base + b, batch)
+        for dst, row, edge in ((0, base - 1, 0), (group + 1, base + group, rows - group)):
+            @pl.when(base != edge)
+            def _():
+                shift(pl.ds(dst, 1), row, 1)
+
+            @pl.when(base == edge)
+            def _():
+                x3[dst] = jnp.zeros(x3.shape[1:], BF)
+
+    loads[0].wait()
 
     def forward(p, pf, pt):
         d = pf * tiles + pt
@@ -204,10 +235,11 @@
         pf = (face + g % faces) % faces
         ph = (tile // half + 1 + side) % 2
         base = (pf * tiles + ph * half) * owned
+        frame(base)
         total = jnp.zeros((group * width, chan), F32)
         for dy in range(3):
             total += jnp.dot(
-                x3[pl.ds(base + dy, group)].reshape(group * width, 3 * chan),
+                x3[pl.ds(dy, group)].reshape(group * width, 3 * chan),
                 w_ref[dy],
                 preferred_element_type=F32,
             )
@@ -269,6 +301,8 @@
             self_sem.at[1, p],
         )
 
+    loads[1].wait()
+    loads[2].wait()
     width_m = min(modes, 256)
     eye = lax.broadcasted_iota(jnp.int32, (width_m, width_m), 0) == lax.broadcasted_iota(
         jnp.int32, (width_m, width_m), 1
@@ -324,11 +358,14 @@
     def _():
         to_left().wait_send()
 
-    for side, end in ((0, 0), (1, tiles - 1)):
+    for side, end, other in ends:
         @pl.when(tile == end)
         def _():
-            for k in range(1, 2 * faces):
-                seam_copy(face * 2 + side, side, k).wait_send()
+            seam_copy(face * 2 + side, 0, face, other).wait_send()
+            for k in range(1, faces):
+                pf = (face + k) % faces
+                seam_copy(face * 2 + side, k, pf, end).wait_send()
+                seam_copy(face * 2 + 1 - side, faces + k - 1, pf, end).wait_send()
 
     for p in range(phases):
         each_peer(lambda pf, pt: forward(p, pf, pt).wait_send())
@@ -348,20 +385,25 @@
     phases = 2 if owned % 2 == 0 else 1
     part = owned // phases
     table = make_table(length, modes)
-    edges = jnp.stack([block_in[:, 0], block_in[:, -1]])
+    group = rows // (2 * faces)
+    anyw = pl.BlockSpec(memory_space=pl.ANY)
     vmem = pl.BlockSpec(memory_space=pltpu.VMEM)
     smem = pl.BlockSpec(memory_space=pltpu.SMEM)
     dma = pltpu.SemaphoreType.DMA
     out = pl.pallas_call(
         functools.partial(kernel, faces, tiles),
         out_shape=jax.ShapeDtypeStruct((rows, width, chan), BF),
-        in_specs=[vmem] * 7 + [smem] * 2,
+        in_specs=[vmem] * 3 + [anyw] * 3 + [smem] * 2,
         out_specs=vmem,
         scratch_shapes=[
+            pltpu.VMEM((3, 3 * chan, chan), BF),
+            pltpu.VMEM((length, 2 * modes), BF),
+            pltpu.VMEM((2 * modes, length), BF),
+            pltpu.VMEM((2, rows, chan), BF),
             pltpu.VMEM((2 * faces, rows, chan), BF),
             pltpu.VMEM((2, rows, chan), BF),
             pltpu.VMEM((2, rows, 1, chan), F32),
-            pltpu.VMEM((rows + 2, width, 3 * chan), BF),
+            pltpu.VMEM((group + 2, width, 3 * chan), BF),
             pltpu.VMEM((rows, width, chan), BF),
             pltpu.VMEM((phases, part, length, chan), BF),
             dma((2,)),
@@ -373,20 +415,20 @@
             dma((phases, devices)),
             dma((phases, devices)),
             dma((2, phases)),
+            dma((3,)),
         ],
         compiler_params=pltpu.CompilerParams(
             collective_id=0, has_side_effects=True, vmem_limit_bytes=60 * 1024 * 1024
         ),
     )(
         block_in,
-        edges,
-        conv_weight.reshape(3, 3 * chan, chan),
         norm_gain.reshape(1, chan),
         filter_gain,
+        conv_weight.reshape(3, 3 * chan, chan),
         jnp.asarray(table),
         jnp.asarray(np.ascontiguousarray(table.T)),
-        seam_face,
-        seam_code,
+        seam_face.T,
+        seam_code.T,
     )
     return out[None]
 

time: 124 us -> 116 us (0.935)
  local copies, waits for them, and re-layouts: 8.54 us -> 3.08 us
    unnamed x4 -> x1, local copies, waits for them, and re-layouts: 8.53 us -> 3.08 us
    pallas_call x1, Pallas kernels: 114 us -> 113 us  [per_device(): pl.pallas_call(functools.partial(kernel, faces, tiles), out_shape=jax.Sha...]
where the time goes in v2:
time: 116 us
  Pallas kernels  113 us (97%)
  local copies, waits for them, and re-layouts  3.08 us (3%)
    pallas_call x1, Pallas kernels, per_device(): pl.pallas_call(functools.partial(kernel, faces, tiles), out_shape=jax.Sha...  113 us
    unnamed x1, local copies, waits for them, and re-layouts  3.08 us

profile of v2, /device:TPU:0, one launch (start us, length us, event | category | flops | bytes accessed | tf_op | source)
XLA Modules:
  0.0 115.7 jit_solution(14140379837071781893)
XLA Ops:
  0.0 112.6 %shard_map.82 = bf16[128,32,256]{2,1,0:T(8,128)(2,1)} custom-call(bf16[128,32,256]{2,1,0:T(8,128)(2,1)} %bitcast.7, f32[1,256]{1,0:T(1,128)} %bitcast.9, f32[2,256]{1,0:T(2,128)} %fgain_ref.1, bf16[3,768,256]{2,1,0:T(8,128)(2,1)} %bitcast.8, bf16[1024,512]{1,0:T(8,128)(2,1)} %constant.4.clone.table_hbm, bf16[512,1024]{1,0:T(8,128)(2,1)} %constant.5.clone.tablet_hbm, ...), custom_call_target="tpu_custom_call" | custom-call | tf_op jit(solution)/shard_map/pallas_call | solution.py:393
  112.6 3.1 %copy.10 = bf16[1,128,32,256]{3,2,1,0:T(8,128)(2,1)} copy(bf16[1,128,32,256]{3,2,1,0:T(8,128)(2,1)} %bitcast.6) | data formatting | bytes 4194304

commit v3 on v2

--- a/solution.py
+++ b/solution.py
@@ -22,7 +22,7 @@
 def kernel(
     faces,
     tiles,
-    x_ref,
+    x_hbm,
     gain_ref,
     fgain_ref,
     w_hbm,
@@ -31,6 +31,7 @@
     sface_ref,
     scode_ref,
     out_ref,
+    x_ref,
     w_ref,
     table_ref,
     tablet_ref,
@@ -49,10 +50,9 @@
     recv1,
     send2,
     recv2,
-    self_sem,
     load_sem,
 ):
-    rows, width, chan = x_ref.shape
+    rows, width, chan = x_hbm.shape
     devices = faces * tiles
     owned = rows // devices
     phases, part = cyc.shape[0], cyc.shape[1]
@@ -66,6 +66,15 @@
 
     barrier = pltpu.get_barrier_semaphore()
 
+    loads = [
+        pltpu.make_async_copy(src, dst, load_sem.at[k])
+        for k, (src, dst) in enumerate(
+            ((x_hbm, x_ref), (w_hbm, w_ref), (tablet_hbm, tablet_ref), (table_hbm, table_ref))
+        )
+    ]
+    for load in loads:
+        load.start()
+
     def peer(k):
         side = k // (faces * half)
         rest = k % (faces * half)
@@ -89,21 +98,13 @@
     each_peer(
         lambda pf, pt: pl.semaphore_signal(barrier, inc=1, device_id=(pf, pt), device_id_type=MESH)
     )
-    loads = [
-        pltpu.make_async_copy(src, dst, load_sem.at[k])
-        for k, (src, dst) in enumerate(
-            ((w_hbm, w_ref), (tablet_hbm, tablet_ref), (table_hbm, table_ref))
-        )
-    ]
-    for load in loads:
-        load.start()
-
     def pick(b, carry):
         at = pl.ds(b * 16, 16)
-        edge_ref[0, at] = x_ref[at].astype(F32)[:, 0, :].astype(BF)
-        edge_ref[1, at] = x_ref[at].astype(F32)[:, width - 1, :].astype(BF)
+        edge_ref[0, at] = x_ref[at, 0:16].astype(F32)[:, 0, :].astype(BF)
+        edge_ref[1, at] = x_ref[at, width - 16 : width].astype(F32)[:, 15, :].astype(BF)
         return carry
 
+    loads[0].wait()
     lax.fori_loop(0, rows // 16, pick, 0)
     pl.semaphore_wait(barrier, devices - 1)
 
@@ -197,26 +198,15 @@
             def _():
                 x3[dst] = jnp.zeros(x3.shape[1:], BF)
 
-    loads[0].wait()
+    loads[1].wait()
 
     def forward(p, pf, pt):
         d = pf * tiles + pt
         return pltpu.make_async_remote_copy(
             mixed.at[pl.ds(d * owned + p * part, part)],
             cyc.at[p, :, pl.ds(me * width, width), :],
-            send1.at[p, d],
-            recv1.at[p, me],
-            device_id=(pf, pt),
-            device_id_type=MESH,
-        )
-
-    def forward_wait(p, pf, pt):
-        s = pf * tiles + pt
-        return pltpu.make_async_remote_copy(
-            mixed.at[pl.ds(s * owned + p * part, part)],
-            cyc.at[p, :, pl.ds(s * width, width), :],
-            send1.at[p, s],
-            recv1.at[p, s],
+            send1.at[p],
+            recv1.at[p],
             device_id=(pf, pt),
             device_id_type=MESH,
         )
@@ -225,7 +215,15 @@
         return pltpu.make_async_copy(
             mixed.at[pl.ds(me * owned + p * part, part)],
             cyc.at[p, :, pl.ds(me * width, width), :],
-            self_sem.at[0, p],
+            recv1.at[p],
+        )
+
+    def whole(p, sem):
+        return pltpu.make_async_copy(mixed.at[pl.ds(0, devices * part)], mixed.at[pl.ds(0, devices * part)], sem.at[p])
+
+    def others(p, sem):
+        return pltpu.make_async_copy(
+            mixed.at[pl.ds(0, (devices - 1) * part)], mixed.at[pl.ds(0, (devices - 1) * part)], sem.at[p]
         )
 
     gain = gain_ref[...]
@@ -277,19 +275,8 @@
         return pltpu.make_async_remote_copy(
             cyc.at[p, :, pl.ds(d * width, width), :],
             out_ref.at[pl.ds(me * owned + p * part, part)],
-            send2.at[p, d],
-            recv2.at[p, me],
-            device_id=(pf, pt),
-            device_id_type=MESH,
-        )
-
-    def back_wait(p, pf, pt):
-        s = pf * tiles + pt
-        return pltpu.make_async_remote_copy(
-            cyc.at[p, :, pl.ds(s * width, width), :],
-            out_ref.at[pl.ds(s * owned + p * part, part)],
-            send2.at[p, s],
-            recv2.at[p, s],
+            send2.at[p],
+            recv2.at[p],
             device_id=(pf, pt),
             device_id_type=MESH,
         )
@@ -298,11 +285,11 @@
         return pltpu.make_async_copy(
             cyc.at[p, :, pl.ds(me * width, width), :],
             out_ref.at[pl.ds(me * owned + p * part, part)],
-            self_sem.at[1, p],
-        )
-
-    loads[1].wait()
+            recv2.at[p],
+        )
+
     loads[2].wait()
+    loads[3].wait()
     width_m = min(modes, 256)
     eye = lax.broadcasted_iota(jnp.int32, (width_m, width_m), 0) == lax.broadcasted_iota(
         jnp.int32, (width_m, width_m), 1
@@ -339,8 +326,7 @@
         lax.fori_loop(0, length // piece, add, 0)
 
     for p in range(phases):
-        each_peer(lambda pf, pt: forward_wait(p, pf, pt).wait_recv())
-        forward_self(p).wait()
+        whole(p, recv1).wait()
 
         def one(r, carry):
             filter_row(p, r)
@@ -368,11 +354,25 @@
                 seam_copy(face * 2 + 1 - side, faces + k - 1, pf, end).wait_send()
 
     for p in range(phases):
-        each_peer(lambda pf, pt: forward(p, pf, pt).wait_send())
+        others(p, send1).wait()
     for p in range(phases):
-        each_peer(lambda pf, pt: back_wait(p, pf, pt).wait_recv())
-        each_peer(lambda pf, pt: back(p, pf, pt).wait_send())
-        back_self(p).wait()
+        others(p, send2).wait()
+        whole(p, recv2).wait()
+
+
+def hand_on(src, dst, held, in_sem, out_sem):
+    count = in_sem.shape[0]
+    step = src.shape[0] // count
+    pieces = [pl.ds(k * step, step) for k in range(count)]
+    loads = [pltpu.make_async_copy(src.at[p], held.at[p], in_sem.at[k]) for k, p in enumerate(pieces)]
+    stores = [pltpu.make_async_copy(held.at[p], dst.at[p], out_sem.at[k]) for k, p in enumerate(pieces)]
+    for load in loads:
+        load.start()
+    for load, store in zip(loads, stores):
+        load.wait()
+        store.start()
+    for store in stores:
+        store.wait()
 
 
 def per_device(faces, tiles, field, conv_weight, norm_gain, filter_gain, seam_face, seam_code):
@@ -393,9 +393,10 @@
     out = pl.pallas_call(
         functools.partial(kernel, faces, tiles),
         out_shape=jax.ShapeDtypeStruct((rows, width, chan), BF),
-        in_specs=[vmem] * 3 + [anyw] * 3 + [smem] * 2,
-        out_specs=vmem,
+        in_specs=[anyw] + [vmem] * 2 + [anyw] * 3 + [smem] * 2,
+        out_specs=anyw,
         scratch_shapes=[
+            pltpu.VMEM((rows, width, chan), BF),
             pltpu.VMEM((3, 3 * chan, chan), BF),
             pltpu.VMEM((length, 2 * modes), BF),
             pltpu.VMEM((2 * modes, length), BF),
@@ -410,12 +411,11 @@
             dma((2,)),
             dma((2 * faces,)),
             dma((2 * faces,)),
-            dma((phases, devices)),
-            dma((phases, devices)),
-            dma((phases, devices)),
-            dma((phases, devices)),
-            dma((2, phases)),
-            dma((3,)),
+            dma((phases,)),
+            dma((phases,)),
+            dma((phases,)),
+            dma((phases,)),
+            dma((4,)),
         ],
         compiler_params=pltpu.CompilerParams(
             collective_id=0, has_side_effects=True, vmem_limit_bytes=60 * 1024 * 1024
@@ -430,7 +430,14 @@
         seam_face.T,
         seam_code.T,
     )
-    return out[None]
+    done = pl.pallas_call(
+        hand_on,
+        out_shape=jax.ShapeDtypeStruct((rows, width, chan), BF),
+        in_specs=[anyw],
+        out_specs=anyw,
+        scratch_shapes=[pltpu.VMEM((rows, width, chan), BF), dma((8,)), dma((8,))],
+    )(out)
+    return done[None]
 
 
 def solution(mesh):

time: 116 us -> 109 us (0.940)
  Pallas kernels: 113 us -> 109 us
  local copies, waits for them, and re-layouts: 3.08 us -> 0 us
    pallas_call x1, Pallas kernels: 113 us -> 107 us  [per_device(): pl.pallas_call(functools.partial(kernel, faces, tiles), out_shape=jax.Sha...]
    unnamed x1 -> x0, local copies, waits for them, and re-layouts: 3.08 us -> none
    pallas_call x0 -> x1, Pallas kernels: none -> 2.39 us  [per_device(): pl.pallas_call(hand_on, out_shape=jax.ShapeDtypeStruct((rows, width, chan...]
where the time goes in v3:
time: 109 us
  Pallas kernels  109 us (100%)
    pallas_call x1, Pallas kernels, per_device(): pl.pallas_call(functools.partial(kernel, faces, tiles), out_shape=jax.Sha...  107 us
    pallas_call x1, Pallas kernels, per_device(): pl.pallas_call(hand_on, out_shape=jax.ShapeDtypeStruct((rows, width, chan...  2.39 us

profile of v3, /device:TPU:0, one launch (start us, length us, event | category | flops | bytes accessed | tf_op | source)
XLA Modules:
  0.0 109.3 jit_solution(5705688557923752197)
XLA Ops:
  0.0 106.9 %shard_map.82.src = bf16[128,32,256]{2,1,0:T(8,128)(2,1)} custom-call(bf16[128,32,256]{2,1,0:T(8,128)(2,1)} %bitcast.6, f32[1,256]{1,0:T(1,128)} %bitcast.8, f32[2,256]{1,0:T(2,128)} %fgain_ref.1, bf16[3,768,256]{2,1,0:T(8,128)(2,1)} %bitcast.7, bf16[1024,512]{1,0:T(8,128)(2,1)} %constant.4.clone.table_hbm, bf16[512,1024]{1,0:T(8,128)(2,1)} %constant.5.clone.tablet_hbm, ...), custom_call_target="tpu_custom_call" | custom-call | tf_op jit(solution)/shard_map/pallas_call | solution.py:393
  106.9 2.4 %shard_map.83 = bf16[128,32,256]{2,1,0:T(8,128)(2,1)} custom-call(bf16[128,32,256]{2,1,0:T(8,128)(2,1)} %shard_map.82.src), custom_call_target="tpu_custom_call" | custom-call | tf_op jit(solution)/shard_map/pallas_call | solution.py:433

commit v4 on v3

--- a/solution.py
+++ b/solution.py
@@ -72,8 +72,7 @@
             ((x_hbm, x_ref), (w_hbm, w_ref), (tablet_hbm, tablet_ref), (table_hbm, table_ref))
         )
     ]
-    for load in loads:
-        load.start()
+    loads[0].start()
 
     def peer(k):
         side = k // (faces * half)
@@ -105,6 +104,8 @@
         return carry
 
     loads[0].wait()
+    for load in loads[1:]:
+        load.start()
     lax.fori_loop(0, rows // 16, pick, 0)
     pl.semaphore_wait(barrier, devices - 1)
 
@@ -268,6 +269,7 @@
     for p in range(phases):
         forward_self(p).start()
     for p in range(1, phases):
+        others(p - 1, send1).wait()
         each_peer(lambda pf, pt: forward(p, pf, pt).start())
 
     def back(p, pf, pt):
@@ -353,8 +355,7 @@
                 seam_copy(face * 2 + side, k, pf, end).wait_send()
                 seam_copy(face * 2 + 1 - side, faces + k - 1, pf, end).wait_send()
 
-    for p in range(phases):
-        others(p, send1).wait()
+    others(phases - 1, send1).wait()
     for p in range(phases):
         others(p, send2).wait()
         whole(p, recv2).wait()

time: 109 us -> 109 us (level)
  no operation moved by 1% of the time
where the time goes in v4:
time: 109 us; the launch traced here: 108 us
  Pallas kernels  108 us (99%)
    pallas_call x1, Pallas kernels, per_device(): pl.pallas_call(functools.partial(kernel, faces, tiles), out_shape=jax.Sha...  106 us
    pallas_call x1, Pallas kernels, per_device(): pl.pallas_call(hand_on, out_shape=jax.ShapeDtypeStruct((rows, width, chan...  2.39 us

profile of v4, /device:TPU:0, one launch (start us, length us, event | category | flops | bytes accessed | tf_op | source)
XLA Modules:
  0.0 108.3 jit_solution(7862385941592110618)
XLA Ops:
  0.0 105.9 %shard_map.82.src = bf16[128,32,256]{2,1,0:T(8,128)(2,1)} custom-call(bf16[128,32,256]{2,1,0:T(8,128)(2,1)} %bitcast.6, f32[1,256]{1,0:T(1,128)} %bitcast.8, f32[2,256]{1,0:T(2,128)} %fgain_ref.1, bf16[3,768,256]{2,1,0:T(8,128)(2,1)} %bitcast.7, bf16[1024,512]{1,0:T(8,128)(2,1)} %constant.4.clone.table_hbm, bf16[512,1024]{1,0:T(8,128)(2,1)} %constant.5.clone.tablet_hbm, ...), custom_call_target="tpu_custom_call" | custom-call | tf_op jit(solution)/shard_map/pallas_call | solution.py:394
  106.0 2.4 %shard_map.83 = bf16[128,32,256]{2,1,0:T(8,128)(2,1)} custom-call(bf16[128,32,256]{2,1,0:T(8,128)(2,1)} %shard_map.82.src), custom_call_target="tpu_custom_call" | custom-call | tf_op jit(solution)/shard_map/pallas_call | solution.py:434
